TPU v7x, 32 devices: a whole 2x2x4 slice. The times are simulated.
32 devices in a mesh: ens: 2 (over y), tile: 16 (over z, x, core).
Axes of the slice: x: 2, y: 2, z: 4, core: 2. Of those that a mesh axis runs over, the one named last changes fastest.
Arguments:
- ocean_state: bfloat16 [512, 512, 128], P(('ens', 'tile')), parts along dimension 0, may hold values from -6 to 6
- atm_flux: bfloat16 [8, 16384], P(None, ('ens', 'tile')), parts along dimension 1, may hold values from -6 to 6
- lat_weights: float32 [256, 6], P('tile'), may hold values from -2.5 to 2.5
- lon_weights: bfloat16 [128, 512], replicated, may hold values from -0.5 to 0.5
- flux_proj: bfloat16 [8, 128], replicated, may hold values from -2 to 2
- conv_kernel: bfloat16 [2, 9, 128, 128], replicated, may hold values from -0.1875 to 0.1875
- conv_bias: float32 [2, 128], replicated, may hold values from -3 to 3
- head: bfloat16 [128, 4], replicated, may hold values from -0.5 to 0.5
Outputs:
- ocean_next: bfloat16 [512, 512, 128], P(('ens', 'tile')), parts along dimension 0
- fields: float32 [4, 512, 512], P(None, ('ens', 'tile')), parts along dimension 1
There are 2 independent parts, one for each index of `ens`. A program takes and returns all parts, laid end to end along the dimension named above; an argument that names none is the same for every part. Nothing has to cross between parts.
All inputs are finite; a program needn't handle non-finite values.
Results may differ from a plain program's by a relative error of at most 0.0064.
Values may be sent and summed in bfloat16 or wider, within the bound.
A program may use at most 64 MiB of HBM per device.

v0:
```python
import jax
import jax.numpy as jnp
from jax import lax
from jax.sharding import PartitionSpec as P


def with_halo(block, sides, width):
    for axis, dim in sides:
        count = lax.axis_size(axis)
        forward = [(i, i + 1) for i in range(count - 1)]
        backward = [(target, source) for source, target in forward]
        low = lax.ppermute(
            lax.slice_in_dim(block, block.shape[dim] - width, None, axis=dim), axis, forward
        )
        high = lax.ppermute(lax.slice_in_dim(block, 0, width, axis=dim), axis, backward)
        block = jnp.concatenate([low, block, high], axis=dim)
    return block


def conv_rows(padded, kernel, bias):
    count = padded.shape[0] - 2
    width = padded.shape[1]
    chans = padded.shape[2]
    total = jnp.zeros((count * width, chans), jnp.float32)
    for offset in range(3):
        band = padded[offset : offset + count]
        stacked = jnp.concatenate(
            [jnp.roll(band, 1 - shift_col, axis=1) for shift_col in range(3)], axis=2
        )
        taps = kernel[3 * offset : 3 * offset + 3].reshape(3 * chans, chans)
        total = total + jnp.dot(
            stacked.reshape(count * width, 3 * chans), taps, preferred_element_type=jnp.float32
        )
    return total.reshape(count, width, chans) + bias


def shards(
    ocean_state, atm_flux, lat_weights, lon_weights, flux_proj, conv_kernel, conv_bias, head
):
    rows = ocean_state.shape[0]
    tiles = lax.axis_size("tile")
    nflux = atm_flux.shape[0]
    sectors = atm_flux.reshape(nflux, lon_weights.shape[0] // tiles, -1)
    widened = with_halo(
        lax.all_to_all(sectors, "tile", split_axis=2, concat_axis=1, tiled=True), (("tile", 2),), 1
    )
    across = jnp.einsum("fla,lc->fac", widened, lon_weights, preferred_element_type=jnp.float32)
    mapped = jnp.einsum("fac,ra->frc", across, lat_weights, precision=lax.Precision.HIGHEST)
    mapped = mapped.astype(jnp.bfloat16)
    forcing = jnp.einsum("frc,fk->rck", mapped, flux_proj, preferred_element_type=jnp.float32)
    state = (ocean_state.astype(jnp.float32) + forcing).astype(jnp.bfloat16)
    layers = conv_kernel.shape[0]
    padded = with_halo(state, (("tile", 0),), layers)
    first_row = lax.axis_index("tile") * rows - layers
    for layer in range(layers):
        hidden = conv_rows(padded, conv_kernel[layer], conv_bias[layer])
        state = (padded[1:-1].astype(jnp.float32) + jax.nn.gelu(hidden, approximate=False)).astype(
            jnp.bfloat16
        )
        if layer + 1 < layers:
            global_row = first_row + layer + 1 + jnp.arange(state.shape[0], dtype=jnp.int32)
            inside = (global_row >= 0) & (global_row < rows * tiles)
            state = jnp.where(inside[:, None, None], state, jnp.zeros_like(state))
        padded = state
    fields = jnp.einsum("rck,kj->jrc", state, head, preferred_element_type=jnp.float32)
    return (state, fields)


def solution(mesh):
    in_specs = (
        P(("ens", "tile"), None, None),
        P(None, ("ens", "tile")),
        P("tile", None),
        P(),
        P(),
        P(),
        P(),
        P(),
    )
    out_specs = (P(("ens", "tile"), None, None), P(None, ("ens", "tile"), None))
    return jax.shard_map(shards, mesh=mesh, in_specs=in_specs, out_specs=out_specs, check_vma=False)
```

profile of v0, /device:TPU:1, one launch (start us, length us, event | category | flops | bytes accessed | tf_op | source)
XLA Modules:
  0.0 129.2 jit_solution(3270900774996035177)
XLA Ops:
  0.6 0.0 copy-start
  0.6 0.0 copy-start.5
  0.7 0.9 reshape.70
  1.5 0.1 copy.11
  1.7 0.2 reshape.89
  1.8 12.9 %all_to_all.18 = bf16[16,2,128]{2,1,0:T(2,128)(2,1)S(1)} all-to-all(bf16[16,2,128]{2,1,0:T(2,128)(2,1)S(1)} %reshape.89), channel_id=1, replica_groups=mesh['ens'=2,'tile'=16] {'tile'}, dimensions={0} | all-to-all | bytes 16384 | tf_op jit(solution)/shard_map/all_to_all | solution.py:45
  14.7 0.2 reshape.90
  14.9 0.1 copy.12
  15.0 0.2 all_to_all.16
  15.1 2.7 %collective-permute-start = (bf16[8,128,1]{1,0,2:T(8,128)(2,1)S(1)}, bf16[8,128,1]{1,0,2:T(8,128)(2,1)S(1)}, u32[]{:S(2)}, u32[]{:S(2)}) collective-permute-start(bf16[8,128,1]{1,0,2:T(8,128)(2,1)S(1)} %get-tuple-element.39), channel_id=1, source_target_pairs={{0,1},{1,2},{2,3},{3,4},{4,5},{5,6},{6,7},{7,8},{8,9},{9,10},{10,1... | collective-permute-start | bytes 6152 | tf_op jit(solution)/shard_map/ppermute | solution.py:12
  17.9 1.9 %collective-permute-start.1 = (bf16[8,128,1]{1,0,2:T(8,128)(2,1)S(1)}, bf16[8,128,1]{1,0,2:T(8,128)(2,1)S(1)}, u32[]{:S(2)}, u32[]{:S(2)}) collective-permute-start(bf16[8,128,1]{1,0,2:T(8,128)(2,1)S(1)} %get-tuple-element.40), channel_id=1, source_target_pairs={{1,0},{2,1},{3,2},{4,3},{5,4},{6,5},{7,6},{8,7},{9,8},{10,9},{11,1... | collective-permute-start | bytes 6152 | tf_op jit(solution)/shard_map/ppermute | solution.py:15
  19.8 0.8 slice_bitcast_fusion
  20.6 0.0 collective-permute-done
  20.6 2.2 %collective-permute-done.1 = bf16[8,128,1]{1,0,2:T(8,128)(2,1)S(1)} collective-permute-done((bf16[8,128,1]{1,0,2:T(8,128)(2,1)S(1)}, bf16[8,128,1]{1,0,2:T(8,128)(2,1)S(1)}, u32[]{:S(2)}, u32[]{:S(2)}) %collective-permute-start.1) | collective-permute-done | bytes 2080 | tf_op jit(solution)/shard_map/ppermute | solution.py:15
  22.8 0.0 copy-done
  22.8 0.1 fusion.40
  22.9 1.1 fusion.43
  24.0 2.6 %add_convert_fusion = bf16[16,512,128]{2,1,0:T(8,128)(2,1)S(1)} fusion(bf16[16,512,128]{2,1,0:T(8,128)(2,1)} %param.8, bf16[8,512,16]{1,2,0:T(8,128)(2,1)S(1)} %fusion.43, bf16[8,128]{1,0:T(8,128)(2,1)} %param.12), kind=kOutput, calls=%fused_computation.65 | convolution fusion | flops 19922944 | bytes 4327424 | tf_op jit(solution)/shard_map/frc,fk->rck/dot_general | solution.py:50
  26.7 2.0 %collective-permute-start.2 = (bf16[2,512,128]{2,1,0:T(8,128)(2,1)S(1)}, bf16[2,512,128]{2,1,0:T(8,128)(2,1)S(1)}, u32[]{:S(2)}, u32[]{:S(2)}) collective-permute-start(bf16[2,512,128]{2,1,0:T(8,128)(2,1)S(1)} %get-tuple-element.32), channel_id=1, source_target_pairs={{0,1},{1,2},{2,3},{3,4},{4,5},{5,6},{6,7},{7,8},{8,9},{9,10},{10,1... | collective-permute-start | bytes 786440 | tf_op jit(solution)/shard_map/ppermute | solution.py:12
  28.7 2.4 %collective-permute-start.3 = (bf16[2,512,128]{2,1,0:T(8,128)(2,1)S(1)}, bf16[2,512,128]{2,1,0:T(8,128)(2,1)S(1)}, u32[]{:S(2)}, u32[]{:S(2)}) collective-permute-start(bf16[2,512,128]{2,1,0:T(8,128)(2,1)S(1)} %get-tuple-element.31), channel_id=1, source_target_pairs={{1,0},{2,1},{3,2},{4,3},{5,4},{6,5},{7,6},{8,7},{9,8},{10,9},{11,1... | collective-permute-start | bytes 786440 | tf_op jit(solution)/shard_map/ppermute | solution.py:15
  31.1 0.0 copy-done.5
  31.1 0.8 collective-permute-done.2
  32.0 5.1 %collective-permute-done.3 = bf16[2,512,128]{2,1,0:T(8,128)(2,1)S(1)} collective-permute-done((bf16[2,512,128]{2,1,0:T(8,128)(2,1)S(1)}, bf16[2,512,128]{2,1,0:T(8,128)(2,1)S(1)}, u32[]{:S(2)}, u32[]{:S(2)}) %collective-permute-start.3) | collective-permute-done | bytes 262176 | tf_op jit(solution)/shard_map/ppermute | solution.py:15
  37.1 0.3 pad_maximum_fusion.8
  37.4 0.0 copy-start.2
  37.4 1.4 %fusion.47 = (bf16[18,511,128]{2,1,0:T(8,128)(2,1)S(1)}, bf16[18,511,128]{2,1,0:T(8,128)(2,1)S(1)}) fusion(bf16[20,512,128]{2,1,0:T(8,128)(2,1)S(1)} %pad_maximum_fusion.8), kind=kLoop, calls=%fused_computation.92 | loop fusion | bytes 9418752 | tf_op jit(solution)/shard_map/jit(_roll_static)/slice | solution.py:28
  38.8 0.0 copy-done.2
  38.9 1.7 %fusion.35 = (bf16[18,511,128]{2,1,0:T(8,128)(2,1)S(1)}, bf16[18,511,128]{2,1,0:T(8,128)(2,1)S(1)}, bf16[18,511,128]{2,1,0:T(8,128)(2,1)S(1)}, bf16[18,511,128]{2,1,0:T(8,128)(2,1)S(1)}) fusion(bf16[2,512,128]{2,1,0:T(8,128)(2,1)S(1)} %collective-permute-done.3, bf16[16,512,128]{2,1,0:T(8,128)(2,1)S(1)} %add_convert_fusion, ...), kind=kLoop, calls=%fused_computation.74 | loop fusion | flops 4709376 | bytes 12040192 | tf_op jit(solution)/shard_map/concatenate | solution.py:16
  40.6 8.2 %fusion.9 = bf16[18,512,384]{2,1,0:T(8,128)(2,1)S(1)} fusion(bf16[16,512,128]{2,1,0:T(8,128)(2,1)S(1)} %add_convert_fusion, bf16[2,512,128]{2,1,0:T(8,128)(2,1)S(1)} %collective-permute-done.2, bf16[18,511,128]{2,1,0:T(8,128)(2,1)S(1)} %get-tuple-element.29, bf16[18,511,128]{2,1,0:T(8,128)(2,1)S(1)} %get-tuple-element.30), kind=kLoop, calls=%fused_computation.20 | loop fusion | flops 56623104 | bytes 14146560 | tf_op jit(solution)/shard_map/concatenate | solution.py:27
  48.8 0.0 slice-start
  48.8 2.0 %fusion.54 = f32[9216,128]{1,0:T(8,128)S(1)} fusion(bf16[9216,384]{1,0:T(8,128)(2,1)S(1)} %bitcast.58, bf16[384,128]{1,0:T(8,128)(2,1)S(1)} %bitcast.73), kind=kOutput, calls=%fused_computation.99 | convolution fusion | flops 905969664 | bytes 11894784 | tf_op jit(solution)/shard_map/dot_general | solution.py:31
  50.8 0.0 slice-done
  50.8 34.5 %fusion.1 = (bf16[18,512,384]{2,1,0:T(8,128)(2,1)S(1)}, bf16[18,512,384]{2,1,0:T(8,128)(2,1)S(1)}) fusion(bf16[2,512,128]{2,1,0:T(8,128)(2,1)S(1)} %collective-permute-done.3, bf16[16,512,128]{2,1,0:T(8,128)(2,1)S(1)} %add_convert_fusion, bf16[18,511,128]{2,1,0:T(8,128)(2,1)S(1)} %get-tuple-element.26, bf16[18,511,128]{2,1,0:T(8,128)(2,1)S(1)} %get-tuple-element.25, ...), kind=kLoop, calls=%fused_computation.6 | loop fusion | flops 120324096 | bytes 28555264 | tf_op jit(solution)/shard_map/concatenate | solution.py:27
  85.4 2.1 %convolution_add_fusion.1 = f32[9216,128]{1,0:T(8,128)S(1)} fusion(f32[9216,128]{1,0:T(8,128)S(1)} %fusion.54, bf16[9216,384]{1,0:T(8,128)(2,1)S(1)} %bitcast.60, bf16[384,128]{1,0:T(8,128)(2,1)S(1)} %bitcast.72), kind=kOutput, calls=%fused_computation.1 | convolution fusion | flops 907149312 | bytes 16613376 | tf_op jit(solution)/shard_map/dot_general | solution.py:31
  87.5 0.0 copy-start.3
  87.5 2.0 %convolution_add_fusion = f32[9216,128]{1,0:T(8,128)S(1)} fusion(f32[9216,128]{1,0:T(8,128)S(1)} %convolution_add_fusion.1, bf16[9216,384]{1,0:T(8,128)(2,1)S(1)} %bitcast.59, bf16[384,128]{1,0:T(8,128)(2,1)S(1)} %bitcast.71), kind=kOutput, calls=%fused_computation | convolution fusion | flops 907149312 | bytes 16613376 | tf_op jit(solution)/shard_map/dot_general | solution.py:31
  89.5 0.0 copy-done.3
  89.6 11.1 %broadcast_select_fusion = bf16[18,512,128]{2,1,0:T(8,128)(2,1)S(1)} fusion(pred[18]{0:T(512)(128)(4,1)S(1)} %compare_and_fusion, f32[18,512,128]{2,1,0:T(8,128)S(1)} %bitcast.64, f32[128]{0:T(128)S(1)} %get-tuple-element.42, bf16[20,512,128]{2,1,0:T(8,128)(2,1)S(1)} %copy-done.3), kind=kLoop, calls=%fused_computation.77 | loop fusion | flops 81395712 | bytes 9437714 | tf_op jit(solution)/shard_map/jit(_where)/select_n | solution.py:63
  100.6 3.7 %fusion.49 = (bf16[16,511,128]{2,1,0:T(8,128)(2,1)S(1)}, bf16[16,511,128]{2,1,0:T(8,128)(2,1)S(1)}, bf16[16,511,128]{2,1,0:T(8,128)(2,1)S(1)}, bf16[16,511,128]{...) fusion(bf16[18,512,128]{2,1,0:T(8,128)(2,1)S(1)} %broadcast_select_fusion), kind=kLoop, calls=%fused_computation.94 | loop fusion | bytes 25116672 | tf_op jit(solution)/shard_map/jit(_roll_static)/slice | solution.py:28
  104.4 1.5 %fusion.50 = (bf16[16,512,128]{2,1,0:T(8,128)(2,1)S(1)}, bf16[16,512,128]{2,1,0:T(8,128)(2,1)S(1)}, bf16[16,512,128]{2,1,0:T(8,128)(2,1)S(1)}) fusion(bf16[18,512,128]{2,1,0:T(8,128)(2,1)S(1)} %broadcast_select_fusion), kind=kLoop, calls=%fused_computation.95 | loop fusion | bytes 12582912 | tf_op jit(solution)/shard_map/slice | solution.py:26
  105.9 3.0 %maximum_maximum_fusion = (bf16[16,512,384]{2,1,0:T(8,128)(2,1)S(1)}, bf16[16,512,384]{2,1,0:T(8,128)(2,1)S(1)}) fusion(bf16[16,1,128]{2,1,0:T(2,128)(2,1)S(1)} %get-tuple-element.12, bf16[16,511,128]{2,1,0:T(8,128)(2,1)S(1)} %get-tuple-element.18, bf16[16,512,128]{2,1,0:T(8,128)(2,1)S(1)} %get-tuple-element.21, ...), kind=kLoop, calls=%fused_computation.25 | loop fusion | flops 62914560 | bytes 25165824 | tf_op jit(solution)/shard_map/concatenate | solution.py:27
  108.9 1.8 %fusion.55 = f32[8192,128]{1,0:T(8,128)S(1)} fusion(bf16[8192,384]{1,0:T(8,128)(2,1)S(1)} %bitcast.63, bf16[384,128]{1,0:T(8,128)(2,1)S(1)} %bitcast.70), kind=kOutput, calls=%fused_computation.100 | convolution fusion | flops 805306368 | bytes 10584064 | tf_op jit(solution)/shard_map/dot_general | solution.py:31
  110.7 1.8 %convolution_add_fusion.3 = f32[8192,128]{1,0:T(8,128)S(1)} fusion(f32[8192,128]{1,0:T(8,128)S(1)} %fusion.55, bf16[8192,384]{1,0:T(8,128)(2,1)S(1)} %bitcast.61, bf16[384,128]{1,0:T(8,128)(2,1)S(1)} %bitcast.69), kind=kOutput, calls=%fused_computation.3 | convolution fusion | flops 806354944 | bytes 14778368 | tf_op jit(solution)/shard_map/dot_general | solution.py:31
  112.5 3.8 %maximum_maximum_fusion.2 = bf16[16,512,384]{2,1,0:T(8,128)(2,1)S(1)} fusion(bf16[16,1,128]{2,1,0:T(2,128)(2,1)S(1)} %get-tuple-element.9, bf16[16,511,128]{2,1,0:T(8,128)(2,1)S(1)} %get-tuple-element.15, bf16[16,512,128]{2,1,0:T(8,128)(2,1)S(1)} %get-tuple-element.20, bf16[16,511,128]{2,1,0:T(8,128)(2,1)S(1)} %get-tuple-element.14, ...), kind=kLoop, calls=%fused_computation.27 | loop fusion | flops 31457280 | bytes 12582912 | tf_op jit(solution)/shard_map/concatenate | solution.py:27
  116.3 1.8 %convolution_add_fusion.2 = f32[8192,128]{1,0:T(8,128)S(1)} fusion(f32[8192,128]{1,0:T(8,128)S(1)} %convolution_add_fusion.3, bf16[8192,384]{1,0:T(8,128)(2,1)S(1)} %bitcast.62, bf16[384,128]{1,0:T(8,128)(2,1)S(1)} %bitcast.68), kind=kOutput, calls=%fused_computation.2 | convolution fusion | flops 806354944 | bytes 14778368 | tf_op jit(solution)/shard_map/dot_general | solution.py:31
  118.1 0.0 copy-start.6
  118.1 0.0 copy-start.1
  118.1 9.7 %fusion.26 = bf16[16,512,128]{2,1,0:T(8,128)(2,1)S(1)} fusion(f32[16,512,128]{2,1,0:T(8,128)S(1)} %bitcast.65, f32[128]{0:T(128)S(1)} %get-tuple-element.41, bf16[18,512,128]{2,1,0:T(8,128)(2,1)S(1)} %broadcast_select_fusion), kind=kLoop, calls=%fused_computation.51 | loop fusion | flops 71303168 | bytes 8389120 | tf_op jit(solution)/shard_map/convert_element_type | solution.py:57
  127.8 0.0 copy-done.6
  127.8 0.0 copy-start.4
  127.8 0.6 convolution_bitcast_fusion
  128.5 0.7 copy.13
  129.2 0.0 copy-done.4
  129.2 0.0 copy-done.1
  (6 shorter events, 0.1 us)
Async XLA Ops:
  0.6 22.2 %copy-start = (bf16[128,512]{1,0:T(8,128)(2,1)S(1)}, bf16[128,512]{1,0:T(8,128)(2,1)}, u32[]{:S(2)}) copy-start(bf16[128,512]{1,0:T(8,128)(2,1)} %param.11) | copy-start | bytes 393220
  0.6 30.4 %copy-start.5 = (bf16[2,9,128,128]{3,2,1,0:T(8,128)(2,1)S(1)}, bf16[2,9,128,128]{3,2,1,0:T(8,128)(2,1)}, u32[]{:S(2)}) copy-start(bf16[2,9,128,128]{3,2,1,0:T(8,128)(2,1)} %param.13) | copy-start | bytes 1769476
  15.1 5.4 %collective-permute-start = (bf16[8,128,1]{1,0,2:T(8,128)(2,1)S(1)}, bf16[8,128,1]{1,0,2:T(8,128)(2,1)S(1)}, u32[]{:S(2)}, u32[]{:S(2)}) collective-permute-start(bf16[8,128,1]{1,0,2:T(8,128)(2,1)S(1)} %get-tuple-element.39), channel_id=1, source_target_pairs={{0,1},{1,2},{2,3},{3,4},{4,5},{5,6},{6,7},{7,8},{8,9},{9,10},{10,1... | collective-permute-start | bytes 6152 | tf_op jit(solution)/shard_map/ppermute | solution.py:12
  17.9 4.9 %collective-permute-start.1 = (bf16[8,128,1]{1,0,2:T(8,128)(2,1)S(1)}, bf16[8,128,1]{1,0,2:T(8,128)(2,1)S(1)}, u32[]{:S(2)}, u32[]{:S(2)}) collective-permute-start(bf16[8,128,1]{1,0,2:T(8,128)(2,1)S(1)} %get-tuple-element.40), channel_id=1, source_target_pairs={{1,0},{2,1},{3,2},{4,3},{5,4},{6,5},{7,6},{8,7},{9,8},{10,9},{11,1... | collective-permute-start | bytes 6152 | tf_op jit(solution)/shard_map/ppermute | solution.py:15
  26.7 5.3 %collective-permute-start.2 = (bf16[2,512,128]{2,1,0:T(8,128)(2,1)S(1)}, bf16[2,512,128]{2,1,0:T(8,128)(2,1)S(1)}, u32[]{:S(2)}, u32[]{:S(2)}) collective-permute-start(bf16[2,512,128]{2,1,0:T(8,128)(2,1)S(1)} %get-tuple-element.32), channel_id=1, source_target_pairs={{0,1},{1,2},{2,3},{3,4},{4,5},{5,6},{6,7},{7,8},{8,9},{9,10},{10,1... | collective-permute-start | bytes 786440 | tf_op jit(solution)/shard_map/ppermute | solution.py:12
  28.7 8.4 %collective-permute-start.3 = (bf16[2,512,128]{2,1,0:T(8,128)(2,1)S(1)}, bf16[2,512,128]{2,1,0:T(8,128)(2,1)S(1)}, u32[]{:S(2)}, u32[]{:S(2)}) collective-permute-start(bf16[2,512,128]{2,1,0:T(8,128)(2,1)S(1)} %get-tuple-element.31), channel_id=1, source_target_pairs={{1,0},{2,1},{3,2},{4,3},{5,4},{6,5},{7,6},{8,7},{9,8},{10,9},{11,1... | collective-permute-start | bytes 786440 | tf_op jit(solution)/shard_map/ppermute | solution.py:15
  37.4 1.5 %copy-start.2 = (bf16[20,512,128]{2,1,0:T(8,128)(2,1)}, bf16[20,512,128]{2,1,0:T(8,128)(2,1)S(1)}, u32[]{:S(2)}) copy-start(bf16[20,512,128]{2,1,0:T(8,128)(2,1)S(1)} %pad_maximum_fusion.8) | copy-start | bytes 7864324
  48.8 2.0 %slice-start = ((bf16[20,512,128]{2,1,0:T(8,128)(2,1)}), bf16[18,512,128]{2,1,0:T(8,128)(2,1)S(1)}, s32[]{:S(2)}) async-start(bf16[20,512,128]{2,1,0:T(8,128)(2,1)} %copy-done.2), calls=%async_computation.1 | async-start | bytes 4718592 | tf_op jit(solution)/shard_map/slice | solution.py:57
  87.5 2.0 %copy-start.3 = (bf16[20,512,128]{2,1,0:T(8,128)(2,1)S(1)}, bf16[20,512,128]{2,1,0:T(8,128)(2,1)}, u32[]{:S(2)}) copy-start(bf16[20,512,128]{2,1,0:T(8,128)(2,1)} %copy-done.2) | copy-start | bytes 7864324
  118.1 9.7 %copy-start.6 = (bf16[128,4]{0,1:T(4,128)(2,1)S(1)}, bf16[128,4]{0,1:T(4,128)(2,1)}, u32[]{:S(2)}) copy-start(bf16[128,4]{0,1:T(4,128)(2,1)} %param.15) | copy-start | bytes 3076
  118.1 11.1 %copy-start.1 = (bf16[128,512]{1,0:T(8,128)(2,1)S(1)}, bf16[128,512]{1,0:T(8,128)(2,1)}, u32[]{:S(2)}) copy-start(bf16[128,512]{1,0:T(8,128)(2,1)} %param.11) | copy-start | bytes 393220
  127.8 1.4 %copy-start.4 = (bf16[16,512,128]{2,1,0:T(8,128)(2,1)}, bf16[16,512,128]{2,1,0:T(8,128)(2,1)S(1)}, u32[]{:S(2)}) copy-start(bf16[16,512,128]{2,1,0:T(8,128)(2,1)S(1)} %fusion.26) | copy-start | bytes 6291460
where the time goes:
time: 130 us; the launch traced here: 129 us
  other arithmetic  72.3 us (56%)
  matrix products  16.1 us (12%)
  blocking collectives  12.9 us (10%)
  local copies, waits for them, and re-layouts  9.88 us (8%)
  starting transfers between devices  9 us (7%)
  waiting for transfers between devices  8.14 us (6%)
    concatenate x4, other arithmetic, conv_rows(): jnp.concatenate([jnp.roll(band, 1 - shift_col, axis=1) for shift_col in r...  49.5 us
    all_to_all x1, blocking collectives, shards(): lax.all_to_all(sectors, 'tile', split_axis=2, concat_axis=1, tiled=True)  12.9 us
    dot_general x6, matrix products, conv_rows(): jnp.dot(stacked.reshape(count * width, 3 * chans), taps, preferred_elemen...  11.6 us
    select_n x1, other arithmetic, shards(): state = jnp.where(inside[:, None, None], state, jnp.zeros_like(state))  11.1 us
    convert_element_type x1, other arithmetic, shards(): (padded[1:-1].astype(jnp.float32) + jax.nn.gelu(hidden, approximate=False...  9.68 us
    ppermute x2, waiting for transfers between devices, with_halo(): lax.ppermute(lax.slice_in_dim(block, 0, width, axis=dim), axis, backward)  7.31 us
    slice x3, local copies, waits for them, and re-layouts, conv_rows(): jnp.roll(band, 1 - shift_col, axis=1)  5.2 us
    ppermute x2, starting transfers between devices, with_halo(): lax.ppermute(lax.slice_in_dim(block, block.shape[dim] - width, None, axis...  4.69 us
  transfers between devices with their start and end apart: 4, of which 3 were waited for; matrix products, arithmetic and copies ran while one was open for 1% of the time, Pallas kernels for 0%

commit v1 on v0

v1 whole, which is shorter than its diff:
```python
import functools

import jax
import jax.numpy as jnp
from jax import lax
from jax.experimental import pallas as pl
from jax.experimental.pallas import tpu as pltpu
from jax.sharding import PartitionSpec as P

MESH = pl.DeviceIdType.MESH
HALO = 2
WINDOW = 16
CHUNK = 256


def exchange_kernel(
    tiles, ocean, flux, lat_own, lon, q_out, halo_out,
    sectors, lat_near, send, recv, halo_send, halo_recv, lat_send, lat_recv,
):
    me = lax.axis_index("tile")
    rows, width, _ = ocean.shape
    nflux = flux.shape[0]
    nlon = lon.shape[0]
    per_dev = nlon // tiles
    nlat = flux.shape[1] // per_dev
    band = nlat // tiles
    taps = lat_own.shape[1]

    barrier = pltpu.get_barrier_semaphore()

    def greet(k, carry):
        pl.semaphore_signal(
            barrier, inc=1, device_id={"tile": lax.rem(me + k, tiles)}, device_id_type=MESH
        )
        return carry

    lax.fori_loop(1, tiles, greet, 0)
    pl.semaphore_wait(barrier, tiles - 1)

    def flux_copy(slot, target, sem):
        return pltpu.make_async_remote_copy(
            src_ref=flux, dst_ref=sectors.at[slot], send_sem=send.at[sem], recv_sem=recv.at[slot],
            device_id={"tile": target}, device_id_type=MESH,
        )

    def lat_copy(slot, target):
        return pltpu.make_async_remote_copy(
            src_ref=lat_own, dst_ref=lat_near.at[slot], send_sem=lat_send.at[slot],
            recv_sem=lat_recv.at[slot], device_id={"tile": target}, device_id_type=MESH,
        )

    def halo_copy(slot, target):
        first = rows - HALO if slot == 0 else 0
        return pltpu.make_async_remote_copy(
            src_ref=ocean.at[pl.ds(first, HALO)], dst_ref=halo_out.at[pl.ds(slot * HALO, HALO)],
            send_sem=halo_send.at[slot], recv_sem=halo_recv.at[slot],
            device_id={"tile": target}, device_id_type=MESH,
        )

    after = lax.rem(me + 1, tiles)
    before = lax.rem(me + tiles - 1, tiles)

    def push(k, carry):
        flux_copy(me, lax.rem(me + k, tiles), k).start()
        return carry

    lax.fori_loop(1, tiles, push, 0)

    @pl.when(me < tiles - 1)
    def _():
        lat_copy(0, after).start()
        halo_copy(0, after).start()

    @pl.when(me > 0)
    def _():
        lat_copy(1, before).start()
        halo_copy(1, before).start()

    @pl.when(me == 0)
    def _():
        lat_near[0] = jnp.zeros_like(lat_own)

    @pl.when(me == tiles - 1)
    def _():
        lat_near[1] = jnp.zeros_like(lat_own)

    sectors[me] = flux[...]

    block = max(nlat, 128)
    group = block // nlat
    span = WINDOW * nflux
    low = me * band - band - 1
    row_id = lax.broadcasted_iota(jnp.int32, (span, block), 0)
    lane_id = lax.broadcasted_iota(jnp.int32, (span, block), 1)
    wanted = low + row_id // nflux
    picks = [
        ((lane_id == wanted + h * nlat) & (wanted >= 0) & (wanted < nlat))
        .astype(jnp.float32).astype(jnp.bfloat16)
        for h in range(group)
    ]
    pairs = tiles * nflux
    same_flux = (
        lax.broadcasted_iota(jnp.int32, (span, pairs), 0) % nflux
        == lax.broadcasted_iota(jnp.int32, (span, pairs), 1) % nflux
    )
    place_row = lax.broadcasted_iota(jnp.int32, (pairs, nlon), 0)
    place_lane = lax.broadcasted_iota(jnp.int32, (pairs, nlon), 1)

    def arrived(k, carry):
        source = lax.rem(me + k, tiles)
        flux_copy(source, source, k).wait_recv()
        return carry

    lax.fori_loop(1, tiles, arrived, 0)

    cells = jnp.zeros((span, nlon), jnp.float32)
    for number in range(per_dev):
        start = number // group * block
        piece = sectors[:, :, start : start + block].reshape(pairs, block)
        found = lax.dot_general(
            picks[number % group], piece, (((1,), (1,)), ((), ())),
            preferred_element_type=jnp.float32,
        )
        found = jnp.where(same_flux, found, 0.0).astype(jnp.bfloat16)
        place = (
            (place_lane == place_row // nflux * per_dev + number)
            .astype(jnp.float32).astype(jnp.bfloat16)
        )
        cells = cells + jnp.dot(found, place, preferred_element_type=jnp.float32)
    across = jnp.dot(
        cells.astype(jnp.bfloat16), lon[...], preferred_element_type=jnp.float32
    )

    @pl.when(me > 0)
    def _():
        lat_copy(0, before).wait_recv()

    @pl.when(me < tiles - 1)
    def _():
        lat_copy(1, after).wait_recv()

    weights = [(lat_near[0], rows - HALO + r, 0) for r in range(HALO)]
    weights += [(lat_own[...], r, band) for r in range(rows)]
    weights += [(lat_near[1], r, 2 * band) for r in range(HALO)]
    mapped = []
    for table, r, offset in weights:
        total = None
        for a in range(taps):
            level = (offset + a) * nflux
            term = table[r : r + 1, a : a + 1] * across[level : level + nflux]
            total = term if total is None else total + term
        mapped.append(total)
    q_out[...] = jnp.concatenate(mapped, axis=0).astype(jnp.bfloat16)

    @pl.when(me > 0)
    def _():
        halo_copy(0, before).wait_recv()
        halo_copy(1, before).wait_send()
        lat_copy(1, before).wait_send()

    @pl.when(me < tiles - 1)
    def _():
        halo_copy(1, after).wait_recv()
        halo_copy(0, after).wait_send()
        lat_copy(0, after).wait_send()

    def left(k, carry):
        flux_copy(me, lax.rem(me + k, tiles), k).wait_send()
        return carry

    lax.fori_loop(1, tiles, left, 0)


def gelu(y):
    return 0.5 * y * (1.0 + lax.erf(y * 0.7071067811865476))


def ocean_kernel(
    tiles, ocean, halo, q, proj, kernel, bias, head, next_out, fields_out,
    raw, state, hidden, taps, result, in_sem, out_sem,
):
    me = lax.axis_index("tile")
    rows, width, chans = ocean.shape
    nflux = proj.shape[0]
    layers = kernel.shape[0]
    pairs = rows // 2
    nfields = head.shape[0]
    wide = 3 * chans

    def fetch(p):
        return pltpu.make_async_copy(
            ocean.at[pl.ds(2 * p - 2, 2)], raw.at[pl.ds(2 * p, 2)], in_sem.at[p]
        )

    def fetch_halo(slot):
        p = slot * (pairs + 1)
        return pltpu.make_async_copy(
            halo.at[pl.ds(slot * HALO, HALO)], raw.at[pl.ds(2 * p, 2)], in_sem.at[p]
        )

    fetch_halo(0).start()
    for p in range(1, pairs + 1):
        fetch(p).start()
    fetch_halo(1).start()

    zero = jnp.zeros((chans, chans), jnp.bfloat16)
    for layer in range(layers):
        for i in range(4):
            for o in range(2):
                for dx in range(3):
                    dy = i - o
                    tap = kernel[layer, 3 * dy + dx] if 0 <= dy < 3 else zero
                    taps[
                        layer, i * wide + dx * chans : i * wide + (dx + 1) * chans,
                        o * chans : (o + 1) * chans,
                    ] = tap

    spread = jnp.concatenate([proj[...].astype(jnp.float32)] * 2, axis=0)
    spread = jnp.concatenate([spread] * 2, axis=1)
    spread = jnp.where(
        lax.broadcasted_iota(jnp.int32, spread.shape, 0) // nflux
        == lax.broadcasted_iota(jnp.int32, spread.shape, 1) // chans,
        spread, 0.0,
    ).astype(jnp.bfloat16)

    def put(ref, p, o, value):
        lane = o * wide
        ref[p, :, lane : lane + chans] = pltpu.roll(value, 1, 0).astype(jnp.bfloat16)
        ref[p, :, lane + 2 * chans : lane + wide] = pltpu.roll(value, width - 1, 0).astype(
            jnp.bfloat16
        )

    def force(p, carry):
        @pl.when(p == 0)
        def _():
            fetch_halo(0).wait()

        @pl.when(p == pairs + 1)
        def _():
            fetch_halo(1).wait()

        @pl.when((p > 0) & (p <= pairs))
        def _():
            fetch(p).wait()

        forcing = lax.dot_general(
            q[pl.ds(pl.multiple_of(p * 2 * nflux, 2 * nflux), 2 * nflux), :], spread,
            (((0,), (0,)), ((), ())), preferred_element_type=jnp.float32,
        )
        for o in range(2):
            u = raw[2 * p + o].astype(jnp.float32) + forcing[:, o * chans : (o + 1) * chans]
            u = u.astype(jnp.bfloat16)
            state[p, :, o * wide + chans : o * wide + 2 * chans] = u
            put(state, p, o, u.astype(jnp.float32))
        return carry

    lax.fori_loop(0, pairs + 2, force, 0)

    @pl.when(me == 0)
    def _():
        state[0] = jnp.zeros((width, 2 * wide), jnp.bfloat16)

    @pl.when(me == tiles - 1)
    def _():
        state[pairs + 1] = jnp.zeros((width, 2 * wide), jnp.bfloat16)

    def conv(source, j, layer, c):
        near = source[j, c : c + CHUNK, :]
        far = source[j + 1, c : c + CHUNK, :]
        y = jnp.dot(
            jnp.concatenate([near, far], axis=1), taps[layer], preferred_element_type=jnp.float32
        )
        b = bias[layer : layer + 1, :]
        g0 = gelu(y[:, :chans] + b)
        g1 = gelu(y[:, chans:] + b)
        v0 = near[:, wide + chans : wide + 2 * chans].astype(jnp.float32) + g0
        v1 = far[:, chans : 2 * chans].astype(jnp.float32) + g1
        return v0.astype(jnp.bfloat16), v1.astype(jnp.bfloat16)

    def first(j, carry):
        for c in range(0, width, CHUNK):
            v0, v1 = conv(state, j, 0, c)
            hidden[j, c : c + CHUNK, chans : 2 * chans] = v0
            hidden[j, c : c + CHUNK, wide + chans : wide + 2 * chans] = v1
        for o in range(2):
            lane = o * wide + chans
            put(hidden, j, o, hidden[j, :, lane : lane + chans].astype(jnp.float32))
        return carry

    lax.fori_loop(0, pairs + 1, first, 0)

    @pl.when(me == 0)
    def _():
        hidden[0, :, :wide] = jnp.zeros((width, wide), jnp.bfloat16)

    @pl.when(me == tiles - 1)
    def _():
        hidden[pairs, :, wide:] = jnp.zeros((width, wide), jnp.bfloat16)

    def store(m):
        return pltpu.make_async_copy(
            result.at[pl.ds(2 * m, 2)], next_out.at[pl.ds(2 * m, 2)], out_sem.at[m]
        )

    def second(m, carry):
        for c in range(0, width, CHUNK):
            for o, v in enumerate(conv(hidden, m, 1, c)):
                result[2 * m + o, c : c + CHUNK, :] = v
                fields_out[:, 2 * m + o, c : c + CHUNK] = lax.dot_general(
                    head[...], v, (((1,), (1,)), ((), ())), preferred_element_type=jnp.float32
                )
        store(m).start()
        return carry

    lax.fori_loop(0, pairs, second, 0)

    def finish(m, carry):
        store(m).wait()
        return carry

    lax.fori_loop(0, pairs, finish, 0)


def shards(
    ocean_state, atm_flux, lat_weights, lon_weights, flux_proj, conv_kernel, conv_bias, head
):
    rows, width, chans = ocean_state.shape
    tiles = lax.axis_size("tile")
    nflux = atm_flux.shape[0]
    vmem = pl.BlockSpec(memory_space=pltpu.VMEM)
    hbm = pl.BlockSpec(memory_space=pl.ANY)
    pair_sem = pltpu.SemaphoreType.DMA((2,))
    q, halo = pl.pallas_call(
        functools.partial(exchange_kernel, tiles),
        out_shape=(
            jax.ShapeDtypeStruct(((rows + 2 * HALO) * nflux, width), jnp.bfloat16),
            jax.ShapeDtypeStruct((2 * HALO, width, chans), jnp.bfloat16),
        ),
        in_specs=[hbm, vmem, vmem, vmem],
        out_specs=(vmem, hbm),
        scratch_shapes=[
            pltpu.VMEM((tiles,) + atm_flux.shape, jnp.bfloat16),
            pltpu.VMEM((2,) + lat_weights.shape, jnp.float32),
            pltpu.SemaphoreType.DMA((tiles,)),
            pltpu.SemaphoreType.DMA((tiles,)),
            pair_sem, pair_sem, pair_sem, pair_sem,
        ],
        compiler_params=pltpu.CompilerParams(
            collective_id=0, has_side_effects=True, vmem_limit_bytes=48 * 2**20
        ),
        name="exchange",
    )(ocean_state, atm_flux, lat_weights, lon_weights)
    pairs = rows // 2
    wide = 3 * chans
    return pl.pallas_call(
        functools.partial(ocean_kernel, tiles),
        out_shape=(
            jax.ShapeDtypeStruct(ocean_state.shape, jnp.bfloat16),
            jax.ShapeDtypeStruct((head.shape[1], rows, width), jnp.float32),
        ),
        in_specs=[hbm, hbm, vmem, vmem, vmem, vmem, vmem],
        out_specs=(hbm, vmem),
        scratch_shapes=[
            pltpu.VMEM((rows + 2 * HALO, width, chans), jnp.bfloat16),
            pltpu.VMEM((pairs + 2, width, 2 * wide), jnp.bfloat16),
            pltpu.VMEM((pairs + 1, width, 2 * wide), jnp.bfloat16),
            pltpu.VMEM((conv_kernel.shape[0], 4 * wide, 2 * chans), jnp.bfloat16),
            pltpu.VMEM(ocean_state.shape, jnp.bfloat16),
            pltpu.SemaphoreType.DMA((pairs + 2,)),
            pltpu.SemaphoreType.DMA((pairs,)),
        ],
        compiler_params=pltpu.CompilerParams(vmem_limit_bytes=48 * 2**20),
        name="ocean",
    )(ocean_state, halo, q, flux_proj, conv_kernel, conv_bias, head.T)


def solution(mesh):
    in_specs = (
        P(("ens", "tile"), None, None),
        P(None, ("ens", "tile")),
        P("tile", None),
        P(),
        P(),
        P(),
        P(),
        P(),
    )
    out_specs = (P(("ens", "tile"), None, None), P(None, ("ens", "tile"), None))
    return jax.shard_map(shards, mesh=mesh, in_specs=in_specs, out_specs=out_specs, check_vma=False)
```

time: 130 us -> 42.3 us (0.33)
  other arithmetic: 72.3 us -> 0 us
  Pallas kernels: 0 us -> 37.4 us
  matrix products: 16.1 us -> 0 us
  blocking collectives: 12.9 us -> 0 us
  starting transfers between devices: 9 us -> 0 us
  waiting for transfers between devices: 8.14 us -> 0 us
  local copies, waits for them, and re-layouts: 9.88 us -> 3.99 us
    concatenate x7 -> x0, other arithmetic: 51.5 us -> none  [the longest x4 49.5 us: conv_rows(): jnp.concatenate([jnp.roll(band, 1 - shift_col, axis=1) for shift_col in r...]
    pallas_call x0 -> x2, Pallas kernels: none -> 37.4 us  [the longest x1 23.6 us: shards(): pl.pallas_call(functools.partial(ocean_kernel, tiles), out_shape=(jax.Sha...]
    dot_general x10 -> x0, matrix products: 16.1 us -> none  [the longest x6 11.6 us: conv_rows(): jnp.dot(stacked.reshape(count * width, 3 * chans), taps, preferred_elemen...]
    all_to_all x1 -> x0, blocking collectives: 12.9 us -> none  [shards(): lax.all_to_all(sectors, 'tile', split_axis=2, concat_axis=1, tiled=True)]
    select_n x1 -> x0, other arithmetic: 11.1 us -> none  [shards(): state = jnp.where(inside[:, None, None], state, jnp.zeros_like(state))]
    convert_element_type x1 -> x0, other arithmetic: 9.68 us -> none  [shards(): (padded[1:-1].astype(jnp.float32) + jax.nn.gelu(hidden, approximate=False...]
    ppermute x4 -> x0, starting transfers between devices: 9 us -> none  [the longest x2 4.69 us: with_halo(): lax.ppermute(lax.slice_in_dim(block, block.shape[dim] - width, None, axis...]
    ppermute x4 -> x0, waiting for transfers between devices: 8.14 us -> none  [the longest x2 7.31 us: with_halo(): lax.ppermute(lax.slice_in_dim(block, 0, width, axis=dim), axis, backward)]
  transfers between devices with their start and end apart: 4 -> 0, of which waited for: 3 -> 0; matrix products, arithmetic and copies ran while one was open for 1% -> 0% of each run, Pallas kernels for 0% -> 0%
where the time goes in v1:
time: 42.3 us; the launch traced here: 42.1 us
  Pallas kernels  37.4 us (88%)
  local copies, waits for them, and re-layouts  3.99 us (9%)
  between operations  0.7 us (2%)
    pallas_call x1, Pallas kernels, shards(): pl.pallas_call(functools.partial(ocean_kernel, tiles), out_shape=(jax.Sha...  23.6 us
    pallas_call x1, Pallas kernels, shards(): pl.pallas_call(functools.partial(exchange_kernel, tiles), out_shape=(jax....  13.8 us
    unnamed x15, local copies, waits for them, and re-layouts  3.99 us

profile of v1, /device:TPU:1, one launch (start us, length us, event | category | flops | bytes accessed | tf_op | source)
XLA Modules:
  0.0 42.1 jit_solution(1344645726595854093)
XLA Ops:
  0.6 0.0 copy-start.6
  0.6 0.0 copy-start.5
  0.7 0.0 copy-start.4
  0.7 0.8 %copy.10.lat_own = f32[16,6]{1,0:T(8,128)S(1)} copy(f32[16,6]{0,1:T(8,128)} %param.10) | data formatting | bytes 768 | tf_op args[2]
  1.4 0.0 copy-start
  1.4 1.6 %copy-done = bf16[16,512,128]{2,1,0:T(8,128)(2,1)S(1)} copy-done((bf16[16,512,128]{2,1,0:T(8,128)(2,1)S(1)}, bf16[16,512,128]{2,1,0:T(8,128)(2,1)}, u32[]{:S(2)}) %copy-start) | copy-done | bytes 2097176
  3.0 0.0 copy-start.2
  3.0 0.9 %copy-done.2 = bf16[128,512]{1,0:T(8,128)(2,1)S(1)} copy-done((bf16[128,512]{1,0:T(8,128)(2,1)S(1)}, bf16[128,512]{1,0:T(8,128)(2,1)}, u32[]{:S(2)}) %copy-start.2) | copy-done | bytes 131096
  3.9 0.0 copy-start.3
  3.9 0.7 %copy-done.3 = bf16[8,512]{1,0:T(8,128)(2,1)S(1)} copy-done((bf16[8,512]{1,0:T(8,128)(2,1)S(1)}, bf16[8,512]{1,0:T(8,128)(2,1)}, u32[]{:S(2)}) %copy-start.3) | copy-done | bytes 8216
  4.6 0.0 copy-start.1
  4.6 13.8 %exchange.1 = (bf16[160,512]{1,0:T(8,128)(2,1)S(1)}, bf16[4,512,128]{2,1,0:T(8,128)(2,1)S(1)}) custom-call(bf16[16,512,128]{2,1,0:T(8,128)(2,1)S(1)} %copy-done, bf16[8,512]{1,0:T(8,128)(2,1)S(1)} %copy-done.3, f32[16,6]{1,0:T(8,128)S(1)} %copy.10.lat_own, bf16[128,512]{1,0:T(8,128)(2,1)S(1)} %copy-done.2), custom_call_target="tpu_custom_call" | custom-call | tf_op jit(solution)/shard_map/exchange/pallas_call | solution.py:333
  18.4 0.0 copy-done.6
  18.4 0.0 copy-done.5
  18.5 0.0 copy-done.4
  18.5 0.0 copy-done.1
  18.5 23.6 %ocean.4 = (bf16[16,512,128]{2,1,0:T(8,128)(2,1)}, f32[4,16,512]{2,1,0:T(8,128)}) custom-call(bf16[16,512,128]{2,1,0:T(8,128)(2,1)S(1)} %copy-done, bf16[4,512,128]{2,1,0:T(8,128)(2,1)S(1)} %get-tuple-element.4.halo, bf16[160,512]{1,0:T(8,128)(2,1)S(1)} %get-tuple-element.5.q, bf16[8,128]{1,0:T(8,128)(2,1)S(1)} %copy-done.4, ...), custom_call_target="tpu_custom_call" | custom-call | tf_op jit(solution)/shard_map/ocean/pallas_call | solution.py:355
Async XLA Ops:
  0.6 17.8 %copy-start.6 = (bf16[128,4]{0,1:T(4,128)(2,1)S(1)}, bf16[128,4]{0,1:T(4,128)(2,1)}, u32[]{:S(2)}) copy-start(bf16[128,4]{0,1:T(4,128)(2,1)} %param.15) | copy-start | bytes 3076
  0.6 17.8 %copy-start.5 = (f32[2,128]{1,0:T(2,128)S(1)}, f32[2,128]{1,0:T(2,128)}, u32[]{:S(2)}) copy-start(f32[2,128]{1,0:T(2,128)} %bias.1) | copy-start | bytes 3076
  0.7 17.8 %copy-start.4 = (bf16[8,128]{1,0:T(8,128)(2,1)S(1)}, bf16[8,128]{1,0:T(8,128)(2,1)}, u32[]{:S(2)}) copy-start(bf16[8,128]{1,0:T(8,128)(2,1)} %proj.1) | copy-start | bytes 6148
  1.4 1.6 %copy-start = (bf16[16,512,128]{2,1,0:T(8,128)(2,1)S(1)}, bf16[16,512,128]{2,1,0:T(8,128)(2,1)}, u32[]{:S(2)}) copy-start(bf16[16,512,128]{2,1,0:T(8,128)(2,1)} %ocean.5) | copy-start | bytes 6291460
  3.0 0.9 %copy-start.2 = (bf16[128,512]{1,0:T(8,128)(2,1)S(1)}, bf16[128,512]{1,0:T(8,128)(2,1)}, u32[]{:S(2)}) copy-start(bf16[128,512]{1,0:T(8,128)(2,1)} %lon.1) | copy-start | bytes 393220
  3.9 0.7 %copy-start.3 = (bf16[8,512]{1,0:T(8,128)(2,1)S(1)}, bf16[8,512]{1,0:T(8,128)(2,1)}, u32[]{:S(2)}) copy-start(bf16[8,512]{1,0:T(8,128)(2,1)} %flux.1) | copy-start | bytes 24580
  4.6 13.8 %copy-start.1 = (bf16[2,9,128,128]{3,2,1,0:T(8,128)(2,1)S(1)}, bf16[2,9,128,128]{3,2,1,0:T(8,128)(2,1)}, u32[]{:S(2)}) copy-start(bf16[2,9,128,128]{3,2,1,0:T(8,128)(2,1)} %kernel.1) | copy-start | bytes 1769476

commit v2 on v1

--- a/solution.py
+++ b/solution.py
@@ -10,23 +10,30 @@
 MESH = pl.DeviceIdType.MESH
 HALO = 2
 WINDOW = 16
-CHUNK = 256
 
 
 def exchange_kernel(
-    tiles, ocean, flux, lat_own, lon, q_out, halo_out,
-    sectors, lat_near, send, recv, halo_send, halo_recv, lat_send, lat_recv,
+    tiles, ocean, flux, lat_in, lon_in, q_out, halo_out,
+    sectors, lat_near, lat_own, lon, send, recv, halo_send, halo_recv, lat_send, lat_recv,
+    local_sem,
 ):
     me = lax.axis_index("tile")
     rows, width, _ = ocean.shape
     nflux = flux.shape[0]
-    nlon = lon.shape[0]
+    nlon = lon_in.shape[0]
     per_dev = nlon // tiles
     nlat = flux.shape[1] // per_dev
     band = nlat // tiles
-    taps = lat_own.shape[1]
+    taps = lat_in.shape[0]
 
     barrier = pltpu.get_barrier_semaphore()
+    local = [
+        pltpu.make_async_copy(flux, sectors.at[me], local_sem.at[0]),
+        pltpu.make_async_copy(lat_in, lat_own, local_sem.at[1]),
+        pltpu.make_async_copy(lon_in, lon, local_sem.at[2]),
+    ]
+    for copy in local:
+        copy.start()
 
     def greet(k, carry):
         pl.semaphore_signal(
@@ -45,7 +52,7 @@
 
     def lat_copy(slot, target):
         return pltpu.make_async_remote_copy(
-            src_ref=lat_own, dst_ref=lat_near.at[slot], send_sem=lat_send.at[slot],
+            src_ref=lat_in, dst_ref=lat_near.at[slot], send_sem=lat_send.at[slot],
             recv_sem=lat_recv.at[slot], device_id={"tile": target}, device_id_type=MESH,
         )
 
@@ -83,8 +90,6 @@
     @pl.when(me == tiles - 1)
     def _():
         lat_near[1] = jnp.zeros_like(lat_own)
-
-    sectors[me] = flux[...]
 
     block = max(nlat, 128)
     group = block // nlat
@@ -113,6 +118,9 @@
 
     lax.fori_loop(1, tiles, arrived, 0)
 
+    for copy in local:
+        copy.wait()
+
     cells = jnp.zeros((span, nlon), jnp.float32)
     for number in range(per_dev):
         start = number // group * block
@@ -147,7 +155,7 @@
         total = None
         for a in range(taps):
             level = (offset + a) * nflux
-            term = table[r : r + 1, a : a + 1] * across[level : level + nflux]
+            term = table[a : a + 1, r : r + 1] * across[level : level + nflux]
             total = term if total is None else total + term
         mapped.append(total)
     q_out[...] = jnp.concatenate(mapped, axis=0).astype(jnp.bfloat16)
@@ -230,19 +238,10 @@
             jnp.bfloat16
         )
 
-    def force(p, carry):
-        @pl.when(p == 0)
-        def _():
-            fetch_halo(0).wait()
-
-        @pl.when(p == pairs + 1)
-        def _():
-            fetch_halo(1).wait()
-
-        @pl.when((p > 0) & (p <= pairs))
-        def _():
-            fetch(p).wait()
-
+    def force(p):
+        pltpu.make_async_copy(
+            halo.at[pl.ds(0, 2)], raw.at[pl.ds(2 * p, 2)], in_sem.at[p]
+        ).wait()
         forcing = lax.dot_general(
             q[pl.ds(pl.multiple_of(p * 2 * nflux, 2 * nflux), 2 * nflux), :], spread,
             (((0,), (0,)), ((), ())), preferred_element_type=jnp.float32,
@@ -252,21 +251,10 @@
             u = u.astype(jnp.bfloat16)
             state[p, :, o * wide + chans : o * wide + 2 * chans] = u
             put(state, p, o, u.astype(jnp.float32))
-        return carry
-
-    lax.fori_loop(0, pairs + 2, force, 0)
-
-    @pl.when(me == 0)
-    def _():
-        state[0] = jnp.zeros((width, 2 * wide), jnp.bfloat16)
-
-    @pl.when(me == tiles - 1)
-    def _():
-        state[pairs + 1] = jnp.zeros((width, 2 * wide), jnp.bfloat16)
-
-    def conv(source, j, layer, c):
-        near = source[j, c : c + CHUNK, :]
-        far = source[j + 1, c : c + CHUNK, :]
+
+    def conv(source, j, layer, n):
+        near = source[pl.ds(j, n)].reshape(n * width, 2 * wide)
+        far = source[pl.ds(j + 1, n)].reshape(n * width, 2 * wide)
         y = jnp.dot(
             jnp.concatenate([near, far], axis=1), taps[layer], preferred_element_type=jnp.float32
         )
@@ -275,44 +263,55 @@
         g1 = gelu(y[:, chans:] + b)
         v0 = near[:, wide + chans : wide + 2 * chans].astype(jnp.float32) + g0
         v1 = far[:, chans : 2 * chans].astype(jnp.float32) + g1
-        return v0.astype(jnp.bfloat16), v1.astype(jnp.bfloat16)
-
-    def first(j, carry):
-        for c in range(0, width, CHUNK):
-            v0, v1 = conv(state, j, 0, c)
-            hidden[j, c : c + CHUNK, chans : 2 * chans] = v0
-            hidden[j, c : c + CHUNK, wide + chans : wide + 2 * chans] = v1
-        for o in range(2):
+        return v0.astype(jnp.bfloat16).reshape(n, width, chans), v1.astype(jnp.bfloat16).reshape(n, width, chans)
+
+    def first(j, n):
+        for o, v in enumerate(conv(state, j, 0, n)):
             lane = o * wide + chans
-            put(hidden, j, o, hidden[j, :, lane : lane + chans].astype(jnp.float32))
-        return carry
-
-    lax.fori_loop(0, pairs + 1, first, 0)
-
-    @pl.when(me == 0)
-    def _():
-        hidden[0, :, :wide] = jnp.zeros((width, wide), jnp.bfloat16)
-
-    @pl.when(me == tiles - 1)
-    def _():
-        hidden[pairs, :, wide:] = jnp.zeros((width, wide), jnp.bfloat16)
+            for i in range(n):
+                hidden[j + i, :, lane : lane + chans] = v[i]
+                put(hidden, j + i, o, v[i].astype(jnp.float32))
 
     def store(m):
         return pltpu.make_async_copy(
             result.at[pl.ds(2 * m, 2)], next_out.at[pl.ds(2 * m, 2)], out_sem.at[m]
         )
 
-    def second(m, carry):
-        for c in range(0, width, CHUNK):
-            for o, v in enumerate(conv(hidden, m, 1, c)):
-                result[2 * m + o, c : c + CHUNK, :] = v
-                fields_out[:, 2 * m + o, c : c + CHUNK] = lax.dot_general(
-                    head[...], v, (((1,), (1,)), ((), ())), preferred_element_type=jnp.float32
+    def second(m, n):
+        for o, v in enumerate(conv(hidden, m, 1, n)):
+            for i in range(n):
+                result[2 * m + 2 * i + o] = v[i]
+                fields_out[:, 2 * m + 2 * i + o, :] = lax.dot_general(
+                    head[...], v[i], (((1,), (1,)), ((), ())), preferred_element_type=jnp.float32
                 )
-        store(m).start()
-        return carry
-
-    lax.fori_loop(0, pairs, second, 0)
+        for i in range(n):
+            store(m + i).start()
+
+    pl.loop(0, pairs + 2)(force)
+
+    @pl.when(me == 0)
+    def _():
+        state[0] = jnp.zeros((width, 2 * wide), jnp.bfloat16)
+
+    @pl.when(me == tiles - 1)
+    def _():
+        state[pairs + 1] = jnp.zeros((width, 2 * wide), jnp.bfloat16)
+
+    first(0, pairs + 1)
+
+    @pl.when(me == 0)
+    def _():
+        hidden[0, :, :wide] = jnp.zeros((width, wide), jnp.bfloat16)
+
+    @pl.when(me == tiles - 1)
+    def _():
+        hidden[pairs, :, wide:] = jnp.zeros((width, wide), jnp.bfloat16)
+
+    half = pairs // 2
+
+    @pl.loop(0, 2)
+    def _(j):
+        second(half * j, half)
 
     def finish(m, carry):
         store(m).wait()
@@ -321,41 +320,16 @@
     lax.fori_loop(0, pairs, finish, 0)
 
 
-def shards(
-    ocean_state, atm_flux, lat_weights, lon_weights, flux_proj, conv_kernel, conv_bias, head
-):
-    rows, width, chans = ocean_state.shape
-    tiles = lax.axis_size("tile")
-    nflux = atm_flux.shape[0]
+def ocean_step(tiles, ocean, halo, q, proj, kernel, bias, head):
+    rows, width, chans = ocean.shape
     vmem = pl.BlockSpec(memory_space=pltpu.VMEM)
-    hbm = pl.BlockSpec(memory_space=pl.ANY)
-    pair_sem = pltpu.SemaphoreType.DMA((2,))
-    q, halo = pl.pallas_call(
-        functools.partial(exchange_kernel, tiles),
-        out_shape=(
-            jax.ShapeDtypeStruct(((rows + 2 * HALO) * nflux, width), jnp.bfloat16),
-            jax.ShapeDtypeStruct((2 * HALO, width, chans), jnp.bfloat16),
-        ),
-        in_specs=[hbm, vmem, vmem, vmem],
-        out_specs=(vmem, hbm),
-        scratch_shapes=[
-            pltpu.VMEM((tiles,) + atm_flux.shape, jnp.bfloat16),
-            pltpu.VMEM((2,) + lat_weights.shape, jnp.float32),
-            pltpu.SemaphoreType.DMA((tiles,)),
-            pltpu.SemaphoreType.DMA((tiles,)),
-            pair_sem, pair_sem, pair_sem, pair_sem,
-        ],
-        compiler_params=pltpu.CompilerParams(
-            collective_id=0, has_side_effects=True, vmem_limit_bytes=48 * 2**20
-        ),
-        name="exchange",
-    )(ocean_state, atm_flux, lat_weights, lon_weights)
+    hbm = pl.BlockSpec(memory_space=pltpu.HBM)
     pairs = rows // 2
     wide = 3 * chans
     return pl.pallas_call(
         functools.partial(ocean_kernel, tiles),
         out_shape=(
-            jax.ShapeDtypeStruct(ocean_state.shape, jnp.bfloat16),
+            jax.ShapeDtypeStruct(ocean.shape, jnp.bfloat16),
             jax.ShapeDtypeStruct((head.shape[1], rows, width), jnp.float32),
         ),
         in_specs=[hbm, hbm, vmem, vmem, vmem, vmem, vmem],
@@ -364,14 +338,51 @@
             pltpu.VMEM((rows + 2 * HALO, width, chans), jnp.bfloat16),
             pltpu.VMEM((pairs + 2, width, 2 * wide), jnp.bfloat16),
             pltpu.VMEM((pairs + 1, width, 2 * wide), jnp.bfloat16),
-            pltpu.VMEM((conv_kernel.shape[0], 4 * wide, 2 * chans), jnp.bfloat16),
-            pltpu.VMEM(ocean_state.shape, jnp.bfloat16),
+            pltpu.VMEM((kernel.shape[0], 4 * wide, 2 * chans), jnp.bfloat16),
+            pltpu.VMEM(ocean.shape, jnp.bfloat16),
             pltpu.SemaphoreType.DMA((pairs + 2,)),
             pltpu.SemaphoreType.DMA((pairs,)),
         ],
-        compiler_params=pltpu.CompilerParams(vmem_limit_bytes=48 * 2**20),
+        compiler_params=pltpu.CompilerParams(vmem_limit_bytes=60 * 2**20),
         name="ocean",
-    )(ocean_state, halo, q, flux_proj, conv_kernel, conv_bias, head.T)
+    )(ocean, halo, q, proj, kernel, bias, head.T)
+
+
+def shards(
+    ocean_state, atm_flux, lat_weights, lon_weights, flux_proj, conv_kernel, conv_bias, head
+):
+    rows, width, chans = ocean_state.shape
+    tiles = lax.axis_size("tile")
+    nflux = atm_flux.shape[0]
+    vmem = pl.BlockSpec(memory_space=pltpu.VMEM)
+    hbm = pl.BlockSpec(memory_space=pltpu.HBM)
+    pair_sem = pltpu.SemaphoreType.DMA((2,))
+    q, halo = pl.pallas_call(
+        functools.partial(exchange_kernel, tiles),
+        out_shape=(
+            jax.ShapeDtypeStruct(((rows + 2 * HALO) * nflux, width), jnp.bfloat16),
+            jax.ShapeDtypeStruct((2 * HALO, width, chans), jnp.bfloat16),
+        ),
+        in_specs=[hbm, hbm, hbm, hbm],
+        out_specs=(vmem, hbm),
+        scratch_shapes=[
+            pltpu.VMEM((tiles,) + atm_flux.shape, jnp.bfloat16),
+            pltpu.VMEM((2,) + lat_weights.shape[::-1], jnp.float32),
+            pltpu.VMEM(lat_weights.shape[::-1], jnp.float32),
+            pltpu.VMEM(lon_weights.shape, jnp.bfloat16),
+            pltpu.SemaphoreType.DMA((tiles,)),
+            pltpu.SemaphoreType.DMA((tiles,)),
+            pair_sem, pair_sem, pair_sem, pair_sem,
+            pltpu.SemaphoreType.DMA((3,)),
+        ],
+        compiler_params=pltpu.CompilerParams(
+            collective_id=0, has_side_effects=True, vmem_limit_bytes=60 * 2**20
+        ),
+        name="exchange",
+    )(ocean_state, atm_flux, lat_weights.T, lon_weights)
+    return ocean_step(
+        tiles, ocean_state, halo, q, flux_proj, conv_kernel, conv_bias, head
+    )
 
 
 def solution(mesh):

time: 42.3 us -> 33.4 us (0.79)
  Pallas kernels: 37.4 us -> 32.6 us
  local copies, waits for them, and re-layouts: 3.99 us -> 0 us
    pallas_call x1, Pallas kernels: 23.6 us -> 17.9 us  [ocean_step(): pl.pallas_call(functools.partial(ocean_kernel, tiles), out_shape=(jax.Sha...]
    unnamed x15 -> x0, local copies, waits for them, and re-layouts: 3.99 us -> none
    pallas_call x1, Pallas kernels: 13.8 us -> 14.7 us  [shards(): pl.pallas_call(functools.partial(exchange_kernel, tiles), out_shape=(jax....]
where the time goes in v2:
time: 33.4 us; the launch traced here: 33.2 us
  Pallas kernels  32.6 us (98%)
  between operations  0.64 us (2%)
    pallas_call x1, Pallas kernels, ocean_step(): pl.pallas_call(functools.partial(ocean_kernel, tiles), out_shape=(jax.Sha...  17.9 us
    pallas_call x1, Pallas kernels, shards(): pl.pallas_call(functools.partial(exchange_kernel, tiles), out_shape=(jax....  14.7 us

profile of v2, /device:TPU:1, one launch (start us, length us, event | category | flops | bytes accessed | tf_op | source)
XLA Modules:
  0.0 33.2 jit_solution(591035840755284024)
XLA Ops:
  0.6 14.7 %exchange.1 = (bf16[160,512]{1,0:T(8,128)(2,1)}, bf16[4,512,128]{2,1,0:T(8,128)(2,1)}) custom-call(bf16[16,512,128]{2,1,0:T(8,128)(2,1)} %ocean.5, bf16[8,512]{1,0:T(8,128)(2,1)} %flux.1, f32[6,16]{1,0:T(8,128)} %bitcast.2, bf16[128,512]{1,0:T(8,128)(2,1)} %lon_in.1), custom_call_target="tpu_custom_call" | custom-call | tf_op jit(solution)/shard_map/exchange/pallas_call | solution.py:360
  15.4 17.9 %ocean.4 = (bf16[16,512,128]{2,1,0:T(8,128)(2,1)}, f32[4,16,512]{2,1,0:T(8,128)}) custom-call(bf16[16,512,128]{2,1,0:T(8,128)(2,1)} %ocean.5, bf16[4,512,128]{2,1,0:T(8,128)(2,1)} %get-tuple-element.4.halo, bf16[160,512]{1,0:T(8,128)(2,1)} %get-tuple-element.5.q, bf16[8,128]{1,0:T(8,128)(2,1)} %proj.1, bf16[2,9,128,128]{3,2,1,0:T(8,128)(2,1)} %kernel.1, ...), custom_call_target="tpu_custom_call" | custom-call | tf_op jit(solution)/shard_map/ocean/pallas_call | solution.py:329

commit v3 on v2

--- a/solution.py
+++ b/solution.py
@@ -13,22 +13,22 @@
 
 
 def exchange_kernel(
-    tiles, ocean, flux, lat_in, lon_in, q_out, halo_out,
-    sectors, lat_near, lat_own, lon, send, recv, halo_send, halo_recv, lat_send, lat_recv,
+    tiles, ocean, flux_in, lat_in, lon_in, q_out, halo_out,
+    flux, parcels, sectors, lat_near, lat_own, lon, send, recv, halo_send, halo_recv, lat_send, lat_recv,
     local_sem,
 ):
     me = lax.axis_index("tile")
     rows, width, _ = ocean.shape
-    nflux = flux.shape[0]
+    nflux = flux_in.shape[0]
     nlon = lon_in.shape[0]
     per_dev = nlon // tiles
-    nlat = flux.shape[1] // per_dev
+    nlat = flux_in.shape[1] // per_dev
     band = nlat // tiles
     taps = lat_in.shape[0]
 
     barrier = pltpu.get_barrier_semaphore()
     local = [
-        pltpu.make_async_copy(flux, sectors.at[me], local_sem.at[0]),
+        pltpu.make_async_copy(flux_in, flux, local_sem.at[0]),
         pltpu.make_async_copy(lat_in, lat_own, local_sem.at[1]),
         pltpu.make_async_copy(lon_in, lon, local_sem.at[2]),
     ]
@@ -42,11 +42,26 @@
         return carry
 
     lax.fori_loop(1, tiles, greet, 0)
+    local[0].wait()
+    block = per_dev * WINDOW
+    cell = lax.broadcasted_iota(jnp.int32, (flux.shape[1], block), 0)
+    slot_lane = lax.broadcasted_iota(jnp.int32, (flux.shape[1], block), 1)
+    gap = jnp.where(
+        cell // nlat == slot_lane // WINDOW, cell % nlat - slot_lane % WINDOW, -2 * nlat
+    )
+
+    def parcel(target):
+        pick = (gap == target * band - band - 1).astype(jnp.float32).astype(jnp.bfloat16)
+        parcels[target] = jnp.dot(
+            flux[...], pick, preferred_element_type=jnp.float32
+        ).astype(jnp.bfloat16)
+
+    pl.loop(0, tiles)(parcel)
     pl.semaphore_wait(barrier, tiles - 1)
 
     def flux_copy(slot, target, sem):
         return pltpu.make_async_remote_copy(
-            src_ref=flux, dst_ref=sectors.at[slot], send_sem=send.at[sem], recv_sem=recv.at[slot],
+            src_ref=parcels.at[target], dst_ref=sectors.at[slot], send_sem=send.at[sem], recv_sem=recv.at[slot],
             device_id={"tile": target}, device_id_type=MESH,
         )
 
@@ -91,18 +106,12 @@
     def _():
         lat_near[1] = jnp.zeros_like(lat_own)
 
-    block = max(nlat, 128)
-    group = block // nlat
+    sectors[me] = parcels[me]
     span = WINDOW * nflux
-    low = me * band - band - 1
-    row_id = lax.broadcasted_iota(jnp.int32, (span, block), 0)
-    lane_id = lax.broadcasted_iota(jnp.int32, (span, block), 1)
-    wanted = low + row_id // nflux
-    picks = [
-        ((lane_id == wanted + h * nlat) & (wanted >= 0) & (wanted < nlat))
-        .astype(jnp.float32).astype(jnp.bfloat16)
-        for h in range(group)
-    ]
+    lane_gap = (
+        lax.broadcasted_iota(jnp.int32, (span, block), 1)
+        - lax.broadcasted_iota(jnp.int32, (span, block), 0) // nflux
+    )
     pairs = tiles * nflux
     same_flux = (
         lax.broadcasted_iota(jnp.int32, (span, pairs), 0) % nflux
@@ -118,15 +127,15 @@
 
     lax.fori_loop(1, tiles, arrived, 0)
 
-    for copy in local:
+    for copy in local[1:]:
         copy.wait()
 
+    arrivals = sectors[...].reshape(pairs, block)
     cells = jnp.zeros((span, nlon), jnp.float32)
     for number in range(per_dev):
-        start = number // group * block
-        piece = sectors[:, :, start : start + block].reshape(pairs, block)
+        pick = (lane_gap == number * WINDOW).astype(jnp.float32).astype(jnp.bfloat16)
         found = lax.dot_general(
-            picks[number % group], piece, (((1,), (1,)), ((), ())),
+            pick, arrivals, (((1,), (1,)), ((), ())),
             preferred_element_type=jnp.float32,
         )
         found = jnp.where(same_flux, found, 0.0).astype(jnp.bfloat16)
@@ -239,11 +248,8 @@
         )
 
     def force(p):
-        pltpu.make_async_copy(
-            halo.at[pl.ds(0, 2)], raw.at[pl.ds(2 * p, 2)], in_sem.at[p]
-        ).wait()
         forcing = lax.dot_general(
-            q[pl.ds(pl.multiple_of(p * 2 * nflux, 2 * nflux), 2 * nflux), :], spread,
+            q[pl.ds(p * 2 * nflux, 2 * nflux), :], spread,
             (((0,), (0,)), ((), ())), preferred_element_type=jnp.float32,
         )
         for o in range(2):
@@ -287,7 +293,12 @@
         for i in range(n):
             store(m + i).start()
 
-    pl.loop(0, pairs + 2)(force)
+    for p in range(pairs + 2):
+        pltpu.make_async_copy(
+            halo.at[pl.ds(0, 2)], raw.at[pl.ds(2 * p, 2)], in_sem.at[p]
+        ).wait()
+    for p in range(pairs + 2):
+        force(p)
 
     @pl.when(me == 0)
     def _():
@@ -356,6 +367,7 @@
     nflux = atm_flux.shape[0]
     vmem = pl.BlockSpec(memory_space=pltpu.VMEM)
     hbm = pl.BlockSpec(memory_space=pltpu.HBM)
+    parcel = lon_weights.shape[0] // tiles * WINDOW
     pair_sem = pltpu.SemaphoreType.DMA((2,))
     q, halo = pl.pallas_call(
         functools.partial(exchange_kernel, tiles),
@@ -366,7 +378,9 @@
         in_specs=[hbm, hbm, hbm, hbm],
         out_specs=(vmem, hbm),
         scratch_shapes=[
-            pltpu.VMEM((tiles,) + atm_flux.shape, jnp.bfloat16),
+            pltpu.VMEM(atm_flux.shape, jnp.bfloat16),
+            pltpu.VMEM((tiles, nflux, parcel), jnp.bfloat16),
+            pltpu.VMEM((tiles, nflux, parcel), jnp.bfloat16),
             pltpu.VMEM((2,) + lat_weights.shape[::-1], jnp.float32),
             pltpu.VMEM(lat_weights.shape[::-1], jnp.float32),
             pltpu.VMEM(lon_weights.shape, jnp.bfloat16),

time: 33.4 us -> 31.6 us (0.946)
  Pallas kernels: 32.6 us -> 30.8 us
    pallas_call x1, Pallas kernels: 14.7 us -> 13.6 us  [shards(): pl.pallas_call(functools.partial(exchange_kernel, tiles), out_shape=(jax....]
    pallas_call x1, Pallas kernels: 17.9 us -> 17.2 us  [ocean_step(): pl.pallas_call(functools.partial(ocean_kernel, tiles), out_shape=(jax.Sha...]
where the time goes in v3:
time: 31.6 us; the launch traced here: 31.4 us
  Pallas kernels  30.8 us (97%)
  between operations  0.64 us (2%)
    pallas_call x1, Pallas kernels, ocean_step(): pl.pallas_call(functools.partial(ocean_kernel, tiles), out_shape=(jax.Sha...  17.2 us
    pallas_call x1, Pallas kernels, shards(): pl.pallas_call(functools.partial(exchange_kernel, tiles), out_shape=(jax....  13.6 us

profile of v3, /device:TPU:1, one launch (start us, length us, event | category | flops | bytes accessed | tf_op | source)
XLA Modules:
  0.0 31.4 jit_solution(17046687568239448369)
XLA Ops:
  0.6 13.6 %exchange.1 = (bf16[160,512]{1,0:T(8,128)(2,1)}, bf16[4,512,128]{2,1,0:T(8,128)(2,1)}) custom-call(bf16[16,512,128]{2,1,0:T(8,128)(2,1)} %ocean.5, bf16[8,512]{1,0:T(8,128)(2,1)} %flux_in.1, f32[6,16]{1,0:T(8,128)} %bitcast.2, bf16[128,512]{1,0:T(8,128)(2,1)} %lon_in.1), custom_call_target="tpu_custom_call" | custom-call | tf_op jit(solution)/shard_map/exchange/pallas_call | solution.py:372
  14.2 17.2 %ocean.4 = (bf16[16,512,128]{2,1,0:T(8,128)(2,1)}, f32[4,16,512]{2,1,0:T(8,128)}) custom-call(bf16[16,512,128]{2,1,0:T(8,128)(2,1)} %ocean.5, bf16[4,512,128]{2,1,0:T(8,128)(2,1)} %get-tuple-element.4.halo, bf16[160,512]{1,0:T(8,128)(2,1)} %get-tuple-element.5.q, bf16[8,128]{1,0:T(8,128)(2,1)} %proj.1, bf16[2,9,128,128]{3,2,1,0:T(8,128)(2,1)} %kernel.1, ...), custom_call_target="tpu_custom_call" | custom-call | tf_op jit(solution)/shard_map/ocean/pallas_call | solution.py:340

commit v4 on v3

--- a/solution.py
+++ b/solution.py
@@ -86,8 +86,6 @@
         flux_copy(me, lax.rem(me + k, tiles), k).start()
         return carry
 
-    lax.fori_loop(1, tiles, push, 0)
-
     @pl.when(me < tiles - 1)
     def _():
         lat_copy(0, after).start()
@@ -97,6 +95,8 @@
     def _():
         lat_copy(1, before).start()
         halo_copy(1, before).start()
+
+    lax.fori_loop(1, tiles, push, 0)
 
     @pl.when(me == 0)
     def _():

time: 31.6 us -> 32.9 us (1.041); the launches traced: 31.4 us -> 32.3 us
  Pallas kernels: 30.8 us -> 31.6 us
    pallas_call x1, Pallas kernels: 13.6 us -> 14.5 us  [shards(): pl.pallas_call(functools.partial(exchange_kernel, tiles), out_shape=(jax....]
where the time goes in v4:
time: 32.9 us; the launch traced here: 32.3 us
  Pallas kernels  31.6 us (96%)
  between operations  0.64 us (2%)
    pallas_call x1, Pallas kernels, ocean_step(): pl.pallas_call(functools.partial(ocean_kernel, tiles), out_shape=(jax.Sha...  17.2 us
    pallas_call x1, Pallas kernels, shards(): pl.pallas_call(functools.partial(exchange_kernel, tiles), out_shape=(jax....  14.5 us

profile of v4, /device:TPU:1, one launch (start us, length us, event | category | flops | bytes accessed | tf_op | source)
XLA Modules:
  0.0 32.3 jit_solution(16334504904151080780)
XLA Ops:
  0.6 14.5 %exchange.1 = (bf16[160,512]{1,0:T(8,128)(2,1)}, bf16[4,512,128]{2,1,0:T(8,128)(2,1)}) custom-call(bf16[16,512,128]{2,1,0:T(8,128)(2,1)} %ocean.5, bf16[8,512]{1,0:T(8,128)(2,1)} %flux_in.1, f32[6,16]{1,0:T(8,128)} %bitcast.2, bf16[128,512]{1,0:T(8,128)(2,1)} %lon_in.1), custom_call_target="tpu_custom_call" | custom-call | tf_op jit(solution)/shard_map/exchange/pallas_call | solution.py:372
  15.1 17.2 %ocean.4 = (bf16[16,512,128]{2,1,0:T(8,128)(2,1)}, f32[4,16,512]{2,1,0:T(8,128)}) custom-call(bf16[16,512,128]{2,1,0:T(8,128)(2,1)} %ocean.5, bf16[4,512,128]{2,1,0:T(8,128)(2,1)} %get-tuple-element.4.halo, bf16[160,512]{1,0:T(8,128)(2,1)} %get-tuple-element.5.q, bf16[8,128]{1,0:T(8,128)(2,1)} %proj.1, bf16[2,9,128,128]{3,2,1,0:T(8,128)(2,1)} %kernel.1, ...), custom_call_target="tpu_custom_call" | custom-call | tf_op jit(solution)/shard_map/ocean/pallas_call | solution.py:340
